TPU v7x, 128 devices: a whole 4x4x4 slice. The times are simulated.
128 devices in a mesh: ctx: 16 (over y, x), head: 8 (over z, core).
Axes of the slice: x: 4, y: 4, z: 4, core: 2. Of those that a mesh axis runs over, the one named last changes fastest.
Arguments:
- query_input: bfloat16 [16, 1024, 4096], P('ctx', 'head'), may hold values from -6 to 6
- key_input: bfloat16 [16, 1024, 512], P('ctx', 'head'), may hold values from -6 to 6
- value_input: bfloat16 [16, 1024, 512], P('ctx', 'head'), may hold values from -6 to 6
- grad_input: bfloat16 [16, 1024, 4096], P('ctx', 'head'), may hold values from -6 to 6
Outputs:
- attended: bfloat16 [16, 1024, 4096], P('ctx', 'head')
- query_grad: float32 [16, 1024, 4096], P('ctx', 'head')
- key_grad: float32 [16, 1024, 512], P('ctx', 'head')
- value_grad: float32 [16, 1024, 512], P('ctx', 'head')
All inputs are finite; a program needn't handle non-finite values.
Results may differ from a plain program's by a relative error of at most 0.0076.
Values may be sent and summed in bfloat16 or wider, within the bound.
No kernel may reach another device: no remote copies, remote signals or barrier semaphores. Data moves between devices by JAX's collectives and lax.ppermute only.
A program may use at most 192 MiB of HBM per device.

v0:
```python
import math

import jax
import jax.numpy as jnp
from jax import lax
from jax.sharding import PartitionSpec as P

HD = 128


def from_partner(value, axis, apart):
    mask = 2**apart
    pairs = [(source, source ^ mask) for source in range(lax.axis_size(axis))]
    return lax.ppermute(value, axis, pairs)


def sent_together(arrays, axis, dim, along):
    both = jnp.concatenate(arrays, axis=along)
    filled, at, outs = (lax.all_gather(both, axis, axis=dim, tiled=True), 0, [])
    for a in arrays:
        outs.append(lax.slice_in_dim(filled, at, at + a.shape[along], axis=along))
        at += a.shape[along]
    return tuple(outs)


def attend(query_split, grad_split, query_pos, key_all, value_all, key_span, scaling):
    rows, pair_heads, sharing, head_dim = query_split.shape
    block_total = (jnp.max(query_pos) + key_span) // key_span

    def block_scores(begin_row):
        key_block = lax.dynamic_slice_in_dim(key_all, begin_row, key_span, 0).reshape(
            key_span, pair_heads, head_dim
        )
        raw_scores = (
            jnp.einsum("ihgd,jhd->hgij", query_split, key_block, preferred_element_type=jnp.float32)
            * scaling
        )
        allowed = (begin_row + jnp.arange(key_span, dtype=jnp.int32))[None, :] <= query_pos[:, None]
        return (jnp.where(allowed, raw_scores, -jnp.inf), key_block)

    def value_slice(begin_row):
        return lax.dynamic_slice_in_dim(value_all, begin_row, key_span, 0).reshape(
            key_span, pair_heads, head_dim
        )

    def stats_pass(step_num, state_in):
        running_max, running_sum = state_in
        scores, unused = block_scores(step_num * key_span)
        highest = jnp.maximum(running_max, jnp.max(scores, axis=-1))
        rescale = jnp.exp(running_max - highest)
        running_sum = running_sum * rescale + jnp.sum(jnp.exp(scores - highest[..., None]), axis=-1)
        return (highest, running_sum)

    stat_shape = (pair_heads, sharing, rows)
    highest, running_sum = lax.fori_loop(
        0,
        block_total,
        stats_pass,
        (jnp.full(stat_shape, -jnp.inf, jnp.float32), jnp.zeros(stat_shape, jnp.float32)),
    )
    log_total = highest + jnp.log(running_sum)

    def output_pass(step_num, running_out):
        begin_row = step_num * key_span
        scores, unused = block_scores(begin_row)
        weights = jnp.exp(scores - log_total[..., None]).astype(jnp.bfloat16)
        return running_out + jnp.einsum(
            "hgij,jhd->hgid", weights, value_slice(begin_row), preferred_element_type=jnp.float32
        )

    running_out = lax.fori_loop(
        0, block_total, output_pass, jnp.zeros(stat_shape + (head_dim,), jnp.float32)
    )
    attended = running_out.transpose(2, 0, 1, 3).astype(jnp.bfloat16)
    row_dot = jnp.sum(
        grad_split.astype(jnp.float32) * attended.astype(jnp.float32), axis=-1
    ).transpose(1, 2, 0)

    def grad_pass(step_num, state_in):
        begin_row = step_num * key_span
        scores, key_block = block_scores(begin_row)
        value_block = value_slice(begin_row)
        normalized = jnp.exp(scores - log_total[..., None])
        weights = normalized.astype(jnp.bfloat16)
        weight_grad = jnp.einsum(
            "ihgd,jhd->hgij", grad_split, value_block, preferred_element_type=jnp.float32
        )
        score_grad = (normalized * (weight_grad - row_dot[..., None])).astype(jnp.bfloat16)
        query_sum = state_in[0] + jnp.einsum(
            "hgij,jhd->ihgd", score_grad, key_block, preferred_element_type=jnp.float32
        )
        return (query_sum,)

    query_zero = jnp.zeros((rows, pair_heads, sharing, head_dim), jnp.float32)
    initial = (query_zero,)
    gradients = lax.fori_loop(0, block_total, grad_pass, initial)
    sums_out = None
    return (attended, gradients[0], sums_out, log_total, row_dot)


def on_device(query_input, key_input, value_input, grad_input):
    local_rows = query_input.shape[1]
    query_width = query_input.shape[2]
    pair_width = key_input.shape[2]
    pair_heads = pair_width // HD
    sharing = query_width // pair_width
    local_heads = pair_heads * sharing
    block_count = lax.axis_size("ctx")
    block_rows = 2 * local_rows
    all_rows = block_count * block_rows
    key_span = min(512, all_rows)
    scaling = 1.0 / math.sqrt(HD)
    block_index = lax.axis_index("ctx")
    half_index = lax.axis_index("head") % 2
    block_first = block_index * block_rows
    first_row = block_first + half_index * local_rows
    query_local = query_input.reshape(local_rows, query_width)
    grad_local = grad_input.reshape(local_rows, query_width)
    own_pairs = jnp.stack(
        [key_input.reshape(local_rows, pair_width), value_input.reshape(local_rows, pair_width)]
    )
    partner_pairs = from_partner(own_pairs, "head", 0)
    block_pairs = jnp.where(
        half_index == 0,
        jnp.concatenate([own_pairs, partner_pairs], axis=1),
        jnp.concatenate([partner_pairs, own_pairs], axis=1),
    )
    gathered_pairs = lax.all_gather(block_pairs, "ctx", axis=1, tiled=True)
    key_all = gathered_pairs[0]
    value_all = gathered_pairs[1]
    query_split = query_local.reshape(local_rows, pair_heads, sharing, HD)
    grad_split = grad_local.reshape(local_rows, pair_heads, sharing, HD)
    query_pos = first_row + jnp.arange(local_rows, dtype=jnp.int32)
    sums_in = None
    attended, query_sum, sums_out, log_total, row_dot = attend(
        query_split, grad_split, query_pos, key_all, value_all, key_span, scaling
    )
    query_grad = scaling * query_sum
    total_rows = log_total.reshape(local_heads, local_rows).T
    dot_rows = row_dot.reshape(local_heads, local_rows).T
    total_all, dot_all = sent_together((total_rows, dot_rows), "ctx", 0, 1)
    block_keys = block_pairs[0].reshape(block_rows, pair_heads, HD)
    block_values = block_pairs[1].reshape(block_rows, pair_heads, HD)
    key_pos = block_first + jnp.arange(block_rows, dtype=jnp.int32)
    zero_rows = jnp.zeros((block_rows, pair_width), jnp.float32)
    query_piece, grad_piece = sent_together((query_local, grad_local), "ctx", 0, 1)
    piece_rows = query_piece.shape[0]
    query_span = math.gcd(piece_rows, 512)
    span_total = piece_rows // query_span

    def one_block(step_num, sums_in):
        offset = step_num * query_span
        gathered_index = offset + jnp.arange(query_span, dtype=jnp.int32)
        row_pos = (
            gathered_index // local_rows * block_rows
            + half_index * local_rows
            + gathered_index % local_rows
        )

        def accumulate(sums_now):
            query_block = lax.dynamic_slice_in_dim(query_piece, offset, query_span, 0).reshape(
                query_span, pair_heads, sharing, HD
            )
            grad_block = lax.dynamic_slice_in_dim(grad_piece, offset, query_span, 0).reshape(
                query_span, pair_heads, sharing, HD
            )
            total_block = lax.dynamic_slice_in_dim(total_all, offset, query_span, 0).T.reshape(
                pair_heads, sharing, query_span
            )
            dot_block = lax.dynamic_slice_in_dim(dot_all, offset, query_span, 0).T.reshape(
                pair_heads, sharing, query_span
            )
            raw_scores = (
                jnp.einsum(
                    "ihgd,jhd->hgij", query_block, block_keys, preferred_element_type=jnp.float32
                )
                * scaling
            )
            allowed = key_pos[None, :] <= row_pos[:, None]
            normalized = jnp.exp(jnp.where(allowed, raw_scores, -jnp.inf) - total_block[..., None])
            weights = normalized.astype(jnp.bfloat16)
            weight_grad = jnp.einsum(
                "ihgd,jhd->hgij", grad_block, block_values, preferred_element_type=jnp.float32
            )
            score_grad = (normalized * (weight_grad - dot_block[..., None])).astype(jnp.bfloat16)
            key_add = jnp.einsum(
                "hgij,ihgd->jhd", score_grad, query_block, preferred_element_type=jnp.float32
            ).reshape(block_rows, pair_width)
            value_add = jnp.einsum(
                "hgij,ihgd->jhd", weights, grad_block, preferred_element_type=jnp.float32
            ).reshape(block_rows, pair_width)
            return (sums_now[0] + key_add, sums_now[1] + value_add)

        def unchanged(sums_now):
            return sums_now

        return lax.cond(jnp.max(row_pos) >= block_first, accumulate, unchanged, sums_in)

    key_sum, value_sum = lax.fori_loop(0, span_total, one_block, (zero_rows, zero_rows))
    outgoing = jnp.stack(
        [
            lax.dynamic_slice_in_dim(key_sum, (1 - half_index) * local_rows, local_rows, 0),
            lax.dynamic_slice_in_dim(value_sum, (1 - half_index) * local_rows, local_rows, 0),
        ]
    )
    incoming = from_partner(outgoing.astype(jnp.bfloat16), "head", 0).astype(outgoing.dtype)
    key_mine = (
        lax.dynamic_slice_in_dim(key_sum, half_index * local_rows, local_rows, 0) + incoming[0]
    )
    value_mine = (
        lax.dynamic_slice_in_dim(value_sum, half_index * local_rows, local_rows, 0) + incoming[1]
    )
    key_grad = scaling * key_mine
    return (
        attended.reshape(1, local_rows, query_width),
        query_grad.reshape(1, local_rows, query_width),
        key_grad.reshape(1, local_rows, pair_width),
        value_mine.reshape(1, local_rows, pair_width),
    )


def solution(mesh):
    in_specs = (
        P("ctx", "head", None),
        P("ctx", "head", None),
        P("ctx", "head", None),
        P("ctx", "head", None),
    )
    out_specs = (
        P("ctx", "head", None),
        P("ctx", "head", None),
        P("ctx", "head", None),
        P("ctx", "head", None),
    )
    return jax.shard_map(
        on_device, mesh=mesh, in_specs=in_specs, out_specs=out_specs, check_vma=False
    )
```

profile of v0, /device:TPU:1, one launch (start us, length us, event | category | flops | bytes accessed | tf_op | source)
XLA Modules:
  0.0 464.3 jit_solution(15359233953880189449)
XLA Ops:
  23.0 62.7 %all-gather.3.cloned.1.call-done = bf16[2,4096,512]{2,1,0:T(8,128)(2,1)} async-done(((bf16[2,256,512]{2,1,0:T(8,128)(2,1)}), bf16[2,4096,512]{2,1,0:T(8,128)(2,1)}) %all-gather.3.cloned.1.call-update) | async-done | bytes 8388624 | tf_op jit(solution)/shard_map/all_gather | solution.py:128
  85.7 5.7 %slice_bitcast_fusion = (bf16[4096,512]{1,0:T(8,128)(2,1)}, bf16[4096,512]{1,0:T(8,128)(2,1)}) fusion(bf16[2,4096,512]{2,1,0:T(8,128)(2,1)} %all-gather.3.cloned.1.call-done), kind=kLoop, calls=%fused_computation.84 | loop fusion | bytes 16777216 | tf_op jit(solution)/shard_map/squeeze | solution.py:130
  91.4 6.4 %copy.72 = bf16[4096,512]{0,1:T(8,128)(2,1)} copy(bf16[4096,512]{1,0:T(8,128)(2,1)} %get-tuple-element.831) | data formatting | bytes 8388608
  97.8 6.7 %copy.74 = bf16[4096,512]{0,1:T(8,128)(2,1)} copy(bf16[4096,512]{1,0:T(8,128)(2,1)} %get-tuple-element.830) | data formatting | bytes 8388608
  110.7 7.7 %while.55 = (s32[]{:T(128)}, f32[4,8,128,128]{3,2,1,0:T(8,128)}, s32[]{:T(128)}, bf16[4096,512]{0,1:T(8,128)(2,1)}, bf16[128,4,8,128]{3,0,2,1:T(8,128)(2,1)S(1)}...) while((s32[]{:T(128)}, f32[4,8,128,128]{3,2,1,0:T(8,128)}, ...), condition=%wide.region_6.7_spmd.clone, body=%wide.region_5.6_spmd.clone.sunk | while | flops 1082720896 | bytes 8541367 | solution.py:71
  112.1 6.2 %fusion.108 = f32[4,8,128,128]{3,2,1,0:T(8,128)} fusion(f32[4,8,128,128]{3,2,1,0:T(8,128)} %get-tuple-element.1133, bf16[512,4,128,1]{0,2,3,1:T(8,128)(2,1)S(1)} %bitcast.231, f32[4,8,128]{2,1,0:T(8,128)S(1)} %get-tuple-element.1149, pred[128,512]{0,1:T(8,128)(4,1)S(1)} %broadcast_compare_fusion.8, bf16[512,4,128,1]{0,2,3,1:T(8,128)(2,1)S(1)} %bitcast.232, ...), kind=kOutput, calls=%fused_computation.46.clone.1 | convolution fusion | flops 1082654720 | bytes 6373376 | tf_op jit(solution)/shard_map/while/body/hgij,jhd->hgid/dot_general | solution.py:67
  122.2 109.7 %all_gather.11 = f32[2048,64]{0,1:T(8,128)S(1)} all-gather(f32[128,64]{0,1:T(8,128)S(1)} %pad_maximum_fusion.2), channel_id=1, replica_groups=mesh['ctx'=16,'head'=8] {'ctx'}, dimensions={0}, use_global_device_ids=true | all-gather | bytes 557056 | tf_op jit(solution)/shard_map/all_gather | solution.py:19
  234.3 14.4 %while.56 = (s32[]{:T(128)}, f32[128,4,8,128]{0,3,2,1:T(8,128)}, s32[]{:T(128)}, bf16[4096,512]{0,1:T(8,128)(2,1)}, bf16[128,4,8,128]{3,0,2,1:T(8,128)(2,1)S(1)}...) while((s32[]{:T(128)}, f32[128,4,8,128]{0,3,2,1:T(8,128)}, ...), condition=%wide.region_9.10_spmd.clone, body=%wide.region_8.9_spmd.clone.sunk | while | flops 1623786112 | bytes 31102180 | solution.py:96
  240.3 8.3 %bitcast_add_fusion.4 = f32[128,4,8,128]{0,3,2,1:T(8,128)} fusion(f32[128,4,8,128]{0,3,2,1:T(8,128)} %get-tuple-element.1171, bf16[512,4,128,1]{0,2,3,1:T(8,128)(2,1)S(1)} %bitcast.225, f32[4,512,128,8]{2,1,3,0:T(8,128)} %fusion.115, f32[4,8,128]{2,1,0:T(8,128)S(1)} %get-tuple-element.1192, f32[4,8,128]{2,1,0:T(8,128)S(1)} %get-tuple-element.1189, ...), kind=kOutput, calls=%fused_computation.63.clone.1 | convolution fusion | flops 1086849024 | bytes 14778368 | tf_op jit(solution)/shard_map/while/body/hgij,jhd->ihgd/dot_general | solution.py:89
  248.7 48.5 %all-gather.5.cloned.1.call-done = bf16[2048,8192]{0,1:T(8,128)(2,1)} async-done(((bf16[128,8192]{0,1:T(8,128)(2,1)}), bf16[2048,8192]{0,1:T(8,128)(2,1)}) %all-gather.5.cloned.1.call-update) | async-done | bytes 33554448 | tf_op jit(solution)/shard_map/all_gather | solution.py:19
  297.2 23.5 %fusion.67 = (bf16[2048,4096]{0,1:T(8,128)(2,1)}, bf16[2048,4096]{0,1:T(8,128)(2,1)}) fusion(bf16[2048,8192]{0,1:T(8,128)(2,1)} %all-gather.5.cloned.1.call-done), kind=kLoop, calls=%fused_computation.107 | loop fusion | bytes 67108864 | tf_op jit(solution)/shard_map/slice | solution.py:21
  320.7 129.3 %while.57 = (s32[]{:T(128)}, f32[256,512]{0,1:T(8,128)S(1)}, f32[256,512]{0,1:T(8,128)S(1)}, s32[]{:T(128)}, s32[]{:T(128)}, /*index=5*/bf16[2048,4096]{0,1:T(8,...) while((s32[]{:T(128)}, f32[256,512]{0,1:T(8,128)S(1)}, ...), condition=%wide.region_14.15_spmd.clone.clone, body=%wide.region_10.14_spmd.clone.clone.sunk | while | flops 4337315840 | bytes 174399952 | solution.py:199
  322.0 31.0 %conditional.4 = ((f32[256,512]{0,1:T(8,128)S(1)}, f32[256,512]{0,1:T(8,128)S(1)})) conditional(s32[]{:T(128)} %convert_element_type.67, (f32[256,512]{0,1:T(8,128)S(1)}, f32[256,512]{0,1:T(8,128)S(1)}) %tuple.142, (s32[]{:T(128)}, bf16[2048,4096]{0,1:T(8,128)(2,1)}, s32[]{:T(128)}, s32[512]{0:T(512)S(1)}, bf16[256,4,128]{2,0,1:T(8,128)(2,1)S(1)}, ...), branch_computations={%region_12.12_spmd, %region_13.13_spmd} | conditional | flops 4337303552 | bytes 174396576 | solution.py:197
  332.4 7.7 %fusion.12 = f32[4,128,256,1]{2,1,3,0:T(8,128)S(1)} fusion(bf16[512,4,8,128]{0,3,2,1:T(8,128)(2,1)} %bitcast.222, f32[4,512,8,256]{3,1,2,0:T(8,128)S(1)} %fusion.18, f32[4,8,512]{2,1,0:T(8,128)S(1)} %dynamic-slice_bitcast_fusion.1, pred[512,256]{1,0:T(8,128)(4,1)S(1)} %broadcast_compare_fusion), kind=kOutput, calls=%fused_computation.10 | convolution fusion | flops 1090519040 | bytes 21692416 | tf_op jit(solution)/shard_map/while/body/eval_jaxpr/cond/branch_1_fun/hgij,ihgd->jhd/dot_general | solution.py:189
  341.0 11.8 %fusion.15 = f32[4,128,256,1]{2,1,3,0:T(8,128)S(1)} fusion(bf16[512,4,8,128]{0,3,2,1:T(8,128)(2,1)} %bitcast.221, f32[4,512,8,256]{3,1,2,0:T(8,128)} %copy-done, bf16[512,4,8,128]{0,3,2,1:T(8,128)(2,1)} %bitcast.223, f32[4,8,512]{2,1,0:T(8,128)S(1)} %dynamic-slice_bitcast_fusion, f32[4,8,512]{2,1,0:T(8,128)S(1)} %dynamic-slice_bitcast_fusion.1, ...), kind=kOutput, calls=%fused_computation.12 | convolution fusion | flops 2172649472 | bytes 26214400 | tf_op jit(solution)/shard_map/while/body/eval_jaxpr/cond/branch_1_fun/hgij,ihgd->jhd/dot_general | solution.py:186
  354.4 31.0 %conditional.4 = ((f32[256,512]{0,1:T(8,128)S(1)}, f32[256,512]{0,1:T(8,128)S(1)})) conditional(s32[]{:T(128)} %convert_element_type.67, (f32[256,512]{0,1:T(8,128)S(1)}, f32[256,512]{0,1:T(8,128)S(1)}) %tuple.142, (s32[]{:T(128)}, bf16[2048,4096]{0,1:T(8,128)(2,1)}, s32[]{:T(128)}, s32[512]{0:T(512)S(1)}, bf16[256,4,128]{2,0,1:T(8,128)(2,1)S(1)}, ...), branch_computations={%region_12.12_spmd, %region_13.13_spmd} | conditional | flops 4337303552 | bytes 174396576 | solution.py:197
  364.8 7.7 %fusion.12 = f32[4,128,256,1]{2,1,3,0:T(8,128)S(1)} fusion(bf16[512,4,8,128]{0,3,2,1:T(8,128)(2,1)} %bitcast.222, f32[4,512,8,256]{3,1,2,0:T(8,128)S(1)} %fusion.18, f32[4,8,512]{2,1,0:T(8,128)S(1)} %dynamic-slice_bitcast_fusion.1, pred[512,256]{1,0:T(8,128)(4,1)S(1)} %broadcast_compare_fusion), kind=kOutput, calls=%fused_computation.10 | convolution fusion | flops 1090519040 | bytes 21692416 | tf_op jit(solution)/shard_map/while/body/eval_jaxpr/cond/branch_1_fun/hgij,ihgd->jhd/dot_general | solution.py:189
  373.4 11.8 %fusion.15 = f32[4,128,256,1]{2,1,3,0:T(8,128)S(1)} fusion(bf16[512,4,8,128]{0,3,2,1:T(8,128)(2,1)} %bitcast.221, f32[4,512,8,256]{3,1,2,0:T(8,128)} %copy-done, bf16[512,4,8,128]{0,3,2,1:T(8,128)(2,1)} %bitcast.223, f32[4,8,512]{2,1,0:T(8,128)S(1)} %dynamic-slice_bitcast_fusion, f32[4,8,512]{2,1,0:T(8,128)S(1)} %dynamic-slice_bitcast_fusion.1, ...), kind=kOutput, calls=%fused_computation.12 | convolution fusion | flops 2172649472 | bytes 26214400 | tf_op jit(solution)/shard_map/while/body/eval_jaxpr/cond/branch_1_fun/hgij,ihgd->jhd/dot_general | solution.py:186
  386.7 31.0 %conditional.4 = ((f32[256,512]{0,1:T(8,128)S(1)}, f32[256,512]{0,1:T(8,128)S(1)})) conditional(s32[]{:T(128)} %convert_element_type.67, (f32[256,512]{0,1:T(8,128)S(1)}, f32[256,512]{0,1:T(8,128)S(1)}) %tuple.142, (s32[]{:T(128)}, bf16[2048,4096]{0,1:T(8,128)(2,1)}, s32[]{:T(128)}, s32[512]{0:T(512)S(1)}, bf16[256,4,128]{2,0,1:T(8,128)(2,1)S(1)}, ...), branch_computations={%region_12.12_spmd, %region_13.13_spmd} | conditional | flops 4337303552 | bytes 174396576 | solution.py:197
  397.1 7.7 %fusion.12 = f32[4,128,256,1]{2,1,3,0:T(8,128)S(1)} fusion(bf16[512,4,8,128]{0,3,2,1:T(8,128)(2,1)} %bitcast.222, f32[4,512,8,256]{3,1,2,0:T(8,128)S(1)} %fusion.18, f32[4,8,512]{2,1,0:T(8,128)S(1)} %dynamic-slice_bitcast_fusion.1, pred[512,256]{1,0:T(8,128)(4,1)S(1)} %broadcast_compare_fusion), kind=kOutput, calls=%fused_computation.10 | convolution fusion | flops 1090519040 | bytes 21692416 | tf_op jit(solution)/shard_map/while/body/eval_jaxpr/cond/branch_1_fun/hgij,ihgd->jhd/dot_general | solution.py:189
  405.7 11.8 %fusion.15 = f32[4,128,256,1]{2,1,3,0:T(8,128)S(1)} fusion(bf16[512,4,8,128]{0,3,2,1:T(8,128)(2,1)} %bitcast.221, f32[4,512,8,256]{3,1,2,0:T(8,128)} %copy-done, bf16[512,4,8,128]{0,3,2,1:T(8,128)(2,1)} %bitcast.223, f32[4,8,512]{2,1,0:T(8,128)S(1)} %dynamic-slice_bitcast_fusion, f32[4,8,512]{2,1,0:T(8,128)S(1)} %dynamic-slice_bitcast_fusion.1, ...), kind=kOutput, calls=%fused_computation.12 | convolution fusion | flops 2172649472 | bytes 26214400 | tf_op jit(solution)/shard_map/while/body/eval_jaxpr/cond/branch_1_fun/hgij,ihgd->jhd/dot_general | solution.py:186
  419.0 31.0 %conditional.4 = ((f32[256,512]{0,1:T(8,128)S(1)}, f32[256,512]{0,1:T(8,128)S(1)})) conditional(s32[]{:T(128)} %convert_element_type.67, (f32[256,512]{0,1:T(8,128)S(1)}, f32[256,512]{0,1:T(8,128)S(1)}) %tuple.142, (s32[]{:T(128)}, bf16[2048,4096]{0,1:T(8,128)(2,1)}, s32[]{:T(128)}, s32[512]{0:T(512)S(1)}, bf16[256,4,128]{2,0,1:T(8,128)(2,1)S(1)}, ...), branch_computations={%region_12.12_spmd, %region_13.13_spmd} | conditional | flops 4337303552 | bytes 174396576 | solution.py:197
  429.4 7.7 %fusion.12 = f32[4,128,256,1]{2,1,3,0:T(8,128)S(1)} fusion(bf16[512,4,8,128]{0,3,2,1:T(8,128)(2,1)} %bitcast.222, f32[4,512,8,256]{3,1,2,0:T(8,128)S(1)} %fusion.18, f32[4,8,512]{2,1,0:T(8,128)S(1)} %dynamic-slice_bitcast_fusion.1, pred[512,256]{1,0:T(8,128)(4,1)S(1)} %broadcast_compare_fusion), kind=kOutput, calls=%fused_computation.10 | convolution fusion | flops 1090519040 | bytes 21692416 | tf_op jit(solution)/shard_map/while/body/eval_jaxpr/cond/branch_1_fun/hgij,ihgd->jhd/dot_general | solution.py:189
  438.0 11.8 %fusion.15 = f32[4,128,256,1]{2,1,3,0:T(8,128)S(1)} fusion(bf16[512,4,8,128]{0,3,2,1:T(8,128)(2,1)} %bitcast.221, f32[4,512,8,256]{3,1,2,0:T(8,128)} %copy-done, bf16[512,4,8,128]{0,3,2,1:T(8,128)(2,1)} %bitcast.223, f32[4,8,512]{2,1,0:T(8,128)S(1)} %dynamic-slice_bitcast_fusion, f32[4,8,512]{2,1,0:T(8,128)S(1)} %dynamic-slice_bitcast_fusion.1, ...), kind=kOutput, calls=%fused_computation.12 | convolution fusion | flops 2172649472 | bytes 26214400 | tf_op jit(solution)/shard_map/while/body/eval_jaxpr/cond/branch_1_fun/hgij,ihgd->jhd/dot_general | solution.py:186
  (133 shorter events, 95.0 us)
Async XLA Ops:
  7.2 78.5 %all-gather.3.cloned.1.call-start = ((), (), s32[]{:S(2)}) async-start(), calls=%async_computation | async-start | bytes 8912896 | tf_op jit(solution)/shard_map/all_gather | solution.py:128
  9.0 2.7 collective-permute-start
  12.7 284.4 %all-gather.5.cloned.1.call-start = ((), (), s32[]{:S(2)}) async-start(), calls=%async_computation.1 | async-start | bytes 35651584 | tf_op jit(solution)/shard_map/all_gather | solution.py:19
  234.3 6.0 %copy-start.4 = (bf16[128,4,8,128]{3,0,2,1:T(8,128)(2,1)S(1)}, bf16[128,4,8,128]{3,0,2,1:T(8,128)(2,1)}, u32[]{:S(2)}) copy-start(bf16[128,4,8,128]{3,0,2,1:T(8,128)(2,1)} %get-tuple-element.1191) | copy-start | bytes 3145732 | tf_op jit(solution)/shard_map/while
  328.9 2.4 copy-start.1
  331.4 8.8 %copy-start = (f32[4,512,8,256]{3,1,2,0:T(8,128)}, f32[4,512,8,256]{3,1,2,0:T(8,128)S(1)}, u32[]{:S(2)}) copy-start(f32[4,512,8,256]{3,1,2,0:T(8,128)S(1)} %fusion.18) | copy-start | bytes 50331652 | tf_op jit(solution)/shard_map/while/body/eval_jaxpr/cond
  332.4 8.6 %copy-start.5 = (bf16[256,4,128]{2,0,1:T(8,128)(2,1)S(1)}, bf16[256,4,128]{2,0,1:T(8,128)(2,1)}, u32[]{:S(2)}) copy-start(bf16[256,4,128]{2,0,1:T(8,128)(2,1)} %get-tuple-element.452) | copy-start | bytes 786436 | tf_op jit(solution)/shard_map/while/body/eval_jaxpr/cond
  361.3 2.4 copy-start.1
  363.7 8.8 %copy-start = (f32[4,512,8,256]{3,1,2,0:T(8,128)}, f32[4,512,8,256]{3,1,2,0:T(8,128)S(1)}, u32[]{:S(2)}) copy-start(f32[4,512,8,256]{3,1,2,0:T(8,128)S(1)} %fusion.18) | copy-start | bytes 50331652 | tf_op jit(solution)/shard_map/while/body/eval_jaxpr/cond
  364.8 8.6 %copy-start.5 = (bf16[256,4,128]{2,0,1:T(8,128)(2,1)S(1)}, bf16[256,4,128]{2,0,1:T(8,128)(2,1)}, u32[]{:S(2)}) copy-start(bf16[256,4,128]{2,0,1:T(8,128)(2,1)} %get-tuple-element.452) | copy-start | bytes 786436 | tf_op jit(solution)/shard_map/while/body/eval_jaxpr/cond
  393.6 2.4 copy-start.1
  396.0 8.8 %copy-start = (f32[4,512,8,256]{3,1,2,0:T(8,128)}, f32[4,512,8,256]{3,1,2,0:T(8,128)S(1)}, u32[]{:S(2)}) copy-start(f32[4,512,8,256]{3,1,2,0:T(8,128)S(1)} %fusion.18) | copy-start | bytes 50331652 | tf_op jit(solution)/shard_map/while/body/eval_jaxpr/cond
  397.1 8.6 %copy-start.5 = (bf16[256,4,128]{2,0,1:T(8,128)(2,1)S(1)}, bf16[256,4,128]{2,0,1:T(8,128)(2,1)}, u32[]{:S(2)}) copy-start(bf16[256,4,128]{2,0,1:T(8,128)(2,1)} %get-tuple-element.452) | copy-start | bytes 786436 | tf_op jit(solution)/shard_map/while/body/eval_jaxpr/cond
  425.9 2.4 copy-start.1
  428.3 8.8 %copy-start = (f32[4,512,8,256]{3,1,2,0:T(8,128)}, f32[4,512,8,256]{3,1,2,0:T(8,128)S(1)}, u32[]{:S(2)}) copy-start(f32[4,512,8,256]{3,1,2,0:T(8,128)S(1)} %fusion.18) | copy-start | bytes 50331652 | tf_op jit(solution)/shard_map/while/body/eval_jaxpr/cond
  429.4 8.6 %copy-start.5 = (bf16[256,4,128]{2,0,1:T(8,128)(2,1)S(1)}, bf16[256,4,128]{2,0,1:T(8,128)(2,1)}, u32[]{:S(2)}) copy-start(bf16[256,4,128]{2,0,1:T(8,128)(2,1)} %get-tuple-element.452) | copy-start | bytes 786436 | tf_op jit(solution)/shard_map/while/body/eval_jaxpr/cond
  450.4 2.4 copy-start.2
  451.3 5.2 %collective-permute-start.1 = (bf16[2,128,512]{2,1,0:T(8,128)(2,1)}, bf16[2,128,512]{2,1,0:T(8,128)(2,1)S(1)}, u32[]{:S(2)}, u32[]{:S(2)}) collective-permute-start(bf16[2,128,512]{2,1,0:T(8,128)(2,1)} %pad_maximum_fusion.1), channel_id=1, source_target_pairs={{0,1},{1,0},{2,3},{3,2},{4,5},{5,4},{6,7},{7,6},{8,9},{9,8},{10,11... | collective-permute-start | bytes 786440 | tf_op jit(solution)/shard_map/ppermute | solution.py:14
  452.9 3.7 copy-start.3
Sparse Core Ops, SparseCore 0:
  12.9 72.7 all-gather.2
  87.8 209.3 all-gather.4
where the time goes:
time: 466 us; the launch traced here: 464 us
  waiting for transfers between devices  112 us (24%)
  blocking collectives  110 us (24%)
  matrix products  108 us (23%)
  local copies, waits for them, and re-layouts  99.7 us (21%)
  between operations  14.9 us (3%)
  other arithmetic  13.3 us (3%)
    all_gather x1, blocking collectives, sent_together(): filled, at, outs = (lax.all_gather(both, axis, axis=dim, tiled=True), 0, [])  110 us
    all_gather x1, waiting for transfers between devices, on_device(): gathered_pairs = lax.all_gather(block_pairs, 'ctx', axis=1, tiled=True)  62.7 us
    all_gather x1, waiting for transfers between devices, sent_together(): filled, at, outs = (lax.all_gather(both, axis, axis=dim, tiled=True), 0, [])  48.5 us
    dot_general x4, matrix products, accumulate(): jnp.einsum('hgij,ihgd->jhd', score_grad, query_block, preferred_element_t...  47.2 us
    dot_general x4, matrix products, accumulate(): jnp.einsum('hgij,ihgd->jhd', weights, grad_block, preferred_element_type=...  30.9 us
    slice x2, local copies, waits for them, and re-layouts, sent_together(): outs.append(lax.slice_in_dim(filled, at, at + a.shape[along], axis=along))  24.3 us
    unnamed x16, local copies, waits for them, and re-layouts  21.7 us
    dynamic_slice x4, local copies, waits for them, and re-layouts, accumulate(): lax.dynamic_slice_in_dim(grad_piece, offset, query_span, 0)  17.7 us
  transfers between devices with their start and end apart: 4, of which 3 were waited for; matrix products, arithmetic and copies ran while one was open for 14% of the time, Pallas kernels for 0%

commit v1 on v0

v1 whole, which is shorter than its diff:
```python
import functools
import math

import jax
import jax.numpy as jnp
from jax import lax
from jax.experimental import pallas as pl
from jax.experimental.pallas import tpu as pltpu
from jax.sharding import PartitionSpec as P

HD = 128
TILE = 256
SHARE = 8
BLOCKS = 16
CHUNKS = 1
BF, F32 = jnp.bfloat16, jnp.float32
SCALE = 1.0 / math.sqrt(HD)
SCALE2 = SCALE * math.log2(math.e)
NT = (((1,), (1,)), ((), ()))
NN = (((1,), (0,)), ((), ()))
AXES = ("ctx", "head")
TEAMS = [
    [c * 8 + 2 * z, c * 8 + 2 * z + 1, (15 - c) * 8 + 2 * z, (15 - c) * 8 + 2 * z + 1]
    for c in range(8)
    for z in range(4)
]
PLANES = [[c * 8 + 2 * z + k for c in range(16) for k in range(2)] for z in range(4)]


def dot(a, b, dims):
    return lax.dot_general(a, b, dims, preferred_element_type=F32)


def causal(width, s, fill):
    row = lax.broadcasted_iota(jnp.int32, (TILE, width), 0)
    col = lax.broadcasted_iota(jnp.int32, (TILE, width), 1) % TILE
    return jnp.where(row <= col, s, fill)


def unpack(g, heads, pieces, q_s, do_s):
    for d in range(4):
        src = g ^ d
        for h in range(heads):
            q_s[src // 2, h, src % 2] = pieces[d][0, :, h * HD : (h + 1) * HD]
            do_s[src // 2, h, src % 2] = pieces[d][1, :, h * HD : (h + 1) * HD]


def value_body(heads, first, last, n_ref, p0, p1, p2, p3, k_ref, *rest):
    if not first:
        prev, *rest = rest
    dv_ref, l_ref, q_s, do_s, dva, e_s, m_s = rest
    width = heads * TILE
    most = jnp.maximum(n_ref[0], n_ref[1])
    unpack(n_ref[2], heads, (p0, p1, p2, p3), q_s, do_s)

    @pl.loop(0, most)
    def _(t):
        dva[t] = jnp.zeros((TILE, HD), F32) if first else prev[t]

    @pl.loop(0, 2)
    def _(it):
        n = n_ref[it]
        qb = q_s[it].reshape(width, HD)
        dob = do_s[it].reshape(width, HD)
        s = causal(width, dot(k_ref[n - 1], qb, NT), -jnp.inf)
        m = jnp.max(s, axis=0, keepdims=True) * SCALE2
        e = jnp.exp2(s * SCALE2 - m)
        l = jnp.sum(e, axis=0, keepdims=True)
        e_s[n - 1] = e.astype(BF)
        m_s[n - 1] = m

        def forward(t, carry):
            m, l = carry
            s = dot(k_ref[t], qb, NT)
            m2 = jnp.maximum(m, jnp.max(s, axis=0, keepdims=True) * SCALE2)
            e = jnp.exp2(s * SCALE2 - m2)
            e_s[t] = e.astype(BF)
            m_s[t] = m2
            return m2, l * jnp.exp2(m - m2) + jnp.sum(e, axis=0, keepdims=True)

        m, l = lax.fori_loop(0, n - 1, forward, (m, l))
        total = m + jnp.log2(l)
        l_ref[it] = total

        def backward(t, _):
            p = e_s[t].astype(F32) * jnp.exp2(m_s[t] - total)
            dva[t] += dot(p.astype(BF), dob, NN)
            return 0

        lax.fori_loop(0, n, backward, 0)

    @pl.loop(0, BLOCKS)
    def _(t):
        @pl.when(t < most)
        def _():
            dv_ref[t] = dva[t].astype(dv_ref.dtype)

        @pl.when(t >= most)
        def _():
            dv_ref[t] = jnp.zeros((TILE, HD), dv_ref.dtype)


def key_body(heads, first, last, n_ref, p0, p1, p2, p3, k_ref, v_ref, l_ref, *rest):
    if not first:
        prev, *rest = rest
    dk_ref, r0, r1, r2, r3, q_s, do_s, o_s, dq_s, kt, vt, dka, p_s, acc = rest
    width = heads * TILE
    g = n_ref[2]
    most = jnp.maximum(n_ref[0], n_ref[1])
    unpack(g, heads, (p0, p1, p2, p3), q_s, do_s)

    @pl.loop(0, most)
    def _(t):
        kt[t] = k_ref[t].T
        vt[t] = v_ref[t].T
        dka[t] = jnp.zeros((TILE, HD), F32) if first else prev[t]

    @pl.loop(0, 2)
    def _(it):
        n = n_ref[it]
        qb = q_s[it].reshape(width, HD)
        dob = do_s[it].reshape(width, HD)
        total = l_ref[it]
        p = causal(width, jnp.exp2(dot(k_ref[n - 1], qb, NT) * SCALE2 - total), 0.0).astype(BF)
        p_s[n - 1] = p
        acc[...] = dot(vt[n - 1], p, NN)

        def forward(t, _):
            p = jnp.exp2(dot(k_ref[t], qb, NT) * SCALE2 - total).astype(BF)
            p_s[t] = p
            acc[...] += dot(vt[t], p, NN)
            return 0

        lax.fori_loop(0, n - 1, forward, 0)
        ot = acc[...].astype(BF)
        row_dot = jnp.sum(dob.T.astype(F32) * ot.astype(F32), axis=0, keepdims=True)
        for h in range(heads):
            for half in range(2):
                at = h * TILE + half * HD
                o_s[it, h, half] = ot[:, at : at + HD].T
        acc[...] = jnp.zeros((HD, width), F32)

        def backward(t, _):
            ds = (p_s[t].astype(F32) * (dot(v_ref[t], dob, NT) - row_dot)).astype(BF)
            dka[t] += dot(ds, qb, NN)
            acc[...] += dot(kt[t], ds, NN)
            return 0

        lax.fori_loop(0, n, backward, 0)
        dqt = (acc[...] * SCALE).astype(BF)
        for h in range(heads):
            for half in range(2):
                at = h * TILE + half * HD
                dq_s[it, h, half] = dqt[:, at : at + HD].T

    for d, out in enumerate((r0, r1, r2, r3)):
        src = g ^ d
        for h in range(heads):
            out[0, :, h * HD : (h + 1) * HD] = o_s[src // 2, h, src % 2]
            out[1, :, h * HD : (h + 1) * HD] = dq_s[src // 2, h, src % 2]

    @pl.loop(0, BLOCKS)
    def _(t):
        @pl.when(t < most)
        def _():
            dk_ref[t] = ((dka[t] * SCALE) if last else dka[t]).astype(dk_ref.dtype)

        @pl.when(t >= most)
        def _():
            dk_ref[t] = jnp.zeros((TILE, HD), dk_ref.dtype)


def assemble_body(chunks, n_ref, *refs):
    pieces, (o_ref, dq_ref) = refs[:-2], refs[-2:]
    g = n_ref[2]
    span = SHARE * HD // chunks
    for c in range(chunks):
        for d in range(4):
            at = pl.multiple_of((g ^ d) * (SHARE * HD) + c * span, span)
            o_ref[0, :, pl.ds(at, span)] = pieces[c * 4 + d][0]
            dq_ref[0, :, pl.ds(at, span)] = pieces[c * 4 + d][1].astype(F32)


VM = pl.BlockSpec(memory_space=pltpu.VMEM)
SM = pl.BlockSpec(memory_space=pltpu.SMEM)


def shape(dims, dtype):
    return jax.ShapeDtypeStruct(dims, dtype)


def value_pass(n, pieces, k, prev, last):
    heads = pieces[0].shape[2] // HD
    width = heads * TILE
    first = prev is None
    held = (2, heads, 2, HD, HD)
    args = (n, *pieces, k) + (() if first else (prev,))
    return pl.pallas_call(
        functools.partial(value_body, heads, first, last),
        out_shape=[shape((BLOCKS, TILE, HD), BF if last else F32), shape((2, 1, width), F32)],
        in_specs=[SM] + [VM] * (len(args) - 1),
        out_specs=[VM] * 2,
        scratch_shapes=[
            pltpu.VMEM(held, BF),
            pltpu.VMEM(held, BF),
            pltpu.VMEM((BLOCKS, TILE, HD), F32),
            pltpu.VMEM((BLOCKS, TILE, width), BF),
            pltpu.VMEM((BLOCKS, 1, width), F32),
        ],
        compiler_params=pltpu.CompilerParams(vmem_limit_bytes=50 * 2**20),
        cost_estimate=pl.CostEstimate(
            flops=17 * 4 * 4 * width * TILE * HD, bytes_accessed=2**22, transcendentals=17 * width * TILE
        ),
        name="value_pass",
    )(*args)


def key_pass(n, pieces, k, v, total, prev, last):
    heads = pieces[0].shape[2] // HD
    width = heads * TILE
    first = prev is None
    held = (2, heads, 2, HD, HD)
    args = (n, *pieces, k, v, total) + (() if first else (prev,))
    return pl.pallas_call(
        functools.partial(key_body, heads, first, last),
        out_shape=[shape((BLOCKS, TILE, HD), BF if last else F32)]
        + [shape((2, HD, heads * HD), BF)] * 4,
        in_specs=[SM] + [VM] * (len(args) - 1),
        out_specs=[VM] * 5,
        scratch_shapes=[pltpu.VMEM(held, BF)] * 4
        + [pltpu.VMEM((BLOCKS, HD, TILE), BF)] * 2
        + [
            pltpu.VMEM((BLOCKS, TILE, HD), F32),
            pltpu.VMEM((BLOCKS, TILE, width), BF),
            pltpu.VMEM((HD, width), F32),
        ],
        compiler_params=pltpu.CompilerParams(vmem_limit_bytes=50 * 2**20),
        cost_estimate=pl.CostEstimate(
            flops=17 * 4 * 10 * width * TILE * HD, bytes_accessed=2**22, transcendentals=17 * width * TILE
        ),
        name="key_pass",
    )(*args)


def assemble(n, pieces, rows):
    return pl.pallas_call(
        functools.partial(assemble_body, len(pieces) // 4),
        out_shape=[shape((1, rows, 4 * SHARE * HD), BF), shape((1, rows, 4 * SHARE * HD), F32)],
        in_specs=[SM] + [VM] * len(pieces),
        out_specs=[VM] * 2,
        compiler_params=pltpu.CompilerParams(vmem_limit_bytes=30 * 2**20),
        name="assemble",
    )(n, *pieces)


def team_swap(pieces):
    out = [pieces[0]]
    for d in (1, 2, 3):
        out.append(lax.ppermute(pieces[d], AXES, [(t[i], t[i ^ d]) for t in TEAMS for i in range(4)]))
    return out


def plane_exchange(x):
    return lax.all_to_all(x, AXES, 0, 0, tiled=True, axis_index_groups=PLANES)


def spread(x, rows):
    heads = x.reshape(rows, 2, 1, 2, HD).transpose(1, 2, 3, 0, 4)
    full = jnp.broadcast_to(heads, (2, 8, 2, rows, HD)).reshape(32, rows, HD)
    return plane_exchange(full).reshape(BLOCKS, TILE, HD)


def collect(x, rows):
    parts = plane_exchange(x.reshape(32, rows, HD)).reshape(2, 8, 2, rows, HD)
    return jnp.sum(parts.astype(F32), axis=1).transpose(2, 0, 1, 3).reshape(1, rows, 4 * HD)


def on_device(query_input, key_input, value_input, grad_input):
    c = lax.axis_index("ctx")
    p = jnp.minimum(c, 15 - c)
    g = 2 * (c >> 3) + (lax.axis_index("head") & 1)
    rows = query_input.shape[1]
    n = jnp.stack([p + 1, 16 - p, g]).astype(jnp.int32)
    span = SHARE * HD // CHUNKS
    q, do = query_input[0], grad_input[0]

    def piece(c, d):
        at = (g ^ d) * (SHARE * HD) + c * span
        return jnp.stack([lax.dynamic_slice_in_dim(x, at, span, 1) for x in (q, do)])

    k = spread(key_input, rows)
    inputs = [team_swap([piece(c, d) for d in range(4)]) for c in range(CHUNKS)]
    v = spread(value_input, rows)
    dv, totals = None, []
    for c in range(CHUNKS):
        dv, total = value_pass(n, inputs[c], k, dv, c == CHUNKS - 1)
        totals.append(total)
    value_grad = collect(dv, rows)
    dk, returned = None, []
    for c in range(CHUNKS):
        dk, *pieces = key_pass(n, inputs[c], k, v, totals[c], dk, c == CHUNKS - 1)
        returned += team_swap(pieces)
    key_grad = collect(dk, rows)
    attended, query_grad = assemble(n, returned, rows)
    return attended, query_grad, key_grad, value_grad


def solution(mesh):
    spec = P("ctx", "head", None)
    return jax.shard_map(
        on_device, mesh=mesh, in_specs=(spec,) * 4, out_specs=(spec,) * 4, check_vma=False
    )
```

time: 466 us -> 174 us (0.37)
  blocking collectives: 110 us -> 0 us
  matrix products: 108 us -> 0 us
  local copies, waits for them, and re-layouts: 99.7 us -> 6.5 us
  Pallas kernels: 0 us -> 59.1 us
  waiting for transfers between devices: 112 us -> 66.8 us
  starting transfers between devices: 3.14 us -> 35.7 us
  between operations: 14.9 us -> 0.81 us
  other arithmetic: 13.3 us -> 4.2 us
    all_gather x2 -> x0, waiting for transfers between devices: 111 us -> none  [the longest x1 62.7 us: on_device(): gathered_pairs = lax.all_gather(block_pairs, 'ctx', axis=1, tiled=True)]
    all_gather x1 -> x0, blocking collectives: 110 us -> none  [sent_together(): filled, at, outs = (lax.all_gather(both, axis, axis=dim, tiled=True), 0, [])]
    dot_general x16 -> x0, matrix products: 108 us -> none  [the longest x4 47.2 us: accumulate(): jnp.einsum('hgij,ihgd->jhd', score_grad, query_block, preferred_element_t...]
    pallas_call x0 -> x3, Pallas kernels: none -> 59.1 us  [the longest x1 31.8 us: key_pass(): pl.pallas_call(functools.partial(key_body, heads, first, last), out_shape...]
    ppermute x2 -> x6, waiting for transfers between devices: 1.16 us -> 57.8 us  [team_swap(): lax.ppermute(pieces[d], AXES, [(t[i], t[i ^ d]) for t in TEAMS for i in r...]
    dynamic_slice x11 -> x1, local copies, waits for them, and re-layouts: 31.2 us -> 0.18 us  [piece(): lax.dynamic_slice_in_dim(x, at, span, 1)]
    slice x4 -> x0, local copies, waits for them, and re-layouts: 25.5 us -> none  [the longest x2 24.3 us: sent_together(): outs.append(lax.slice_in_dim(filled, at, at + a.shape[along], axis=along))]
    all_to_all x0 -> x4, starting transfers between devices: none -> 24.7 us  [plane_exchange(): return lax.all_to_all(x, AXES, 0, 0, tiled=True, axis_index_groups=PLANES)]
  transfers between devices with their start and end apart: 4 -> 10, of which waited for: 3 -> 5; matrix products, arithmetic and copies ran while one was open for 14% -> 4% of each run, Pallas kernels for 0% -> 34%
where the time goes in v1:
time: 174 us; the launch traced here: 173 us
  waiting for transfers between devices  66.8 us (38%)
  Pallas kernels  59.1 us (34%)
  starting transfers between devices  35.7 us (21%)
  local copies, waits for them, and re-layouts  6.5 us (4%)
  other arithmetic  4.2 us (2%)
    ppermute x6, waiting for transfers between devices, team_swap(): lax.ppermute(pieces[d], AXES, [(t[i], t[i ^ d]) for t in TEAMS for i in r...  57.8 us
    pallas_call x1, Pallas kernels, key_pass(): pl.pallas_call(functools.partial(key_body, heads, first, last), out_shape...  31.8 us
    pallas_call x1, Pallas kernels, value_pass(): pl.pallas_call(functools.partial(value_body, heads, first, last), out_sha...  24.9 us
    all_to_all x4, starting transfers between devices, plane_exchange(): return lax.all_to_all(x, AXES, 0, 0, tiled=True, axis_index_groups=PLANES)  24.7 us
    ppermute x6, starting transfers between devices, team_swap(): lax.ppermute(pieces[d], AXES, [(t[i], t[i ^ d]) for t in TEAMS for i in r...  11 us
    all_to_all x4, waiting for transfers between devices, plane_exchange(): return lax.all_to_all(x, AXES, 0, 0, tiled=True, axis_index_groups=PLANES)  9.01 us
  transfers between devices with their start and end apart: 10, of which 5 were waited for; matrix products, arithmetic and copies ran while one was open for 4% of the time, Pallas kernels for 34%

profile of v1, /device:TPU:1, one launch (start us, length us, event | category | flops | bytes accessed | tf_op | source)
XLA Modules:
  0.0 173.0 jit_solution(13415145415172079950)
XLA Ops:
  0.7 1.1 reshape.60
  1.8 1.2 broadcast_in_dim.15
  3.0 8.6 %all-to-all-start = ((bf16[32,128,128]{2,1,0:T(8,128)(2,1)}), bf16[32,128,128]{2,1,0:T(8,128)(2,1)}, u32[]{:S(2)}, u32[]{:S(2)}) async-start(bf16[32,128,128]{2,1,0:T(8,128)(2,1)} %bitcast.5), calls=%async_computation | async-start | bytes 2097152 | tf_op jit(solution)/shard_map/all_to_all | solution.py:264
  11.9 0.9 pad_maximum_fusion.2
  12.7 4.8 %collective-permute-start.1 = (bf16[2,128,1024]{2,1,0:T(8,128)(2,1)}, bf16[2,128,1024]{2,1,0:T(8,128)(2,1)S(1)}, u32[]{:S(2)}, u32[]{:S(2)}) collective-permute-start(bf16[2,128,1024]{2,1,0:T(8,128)(2,1)} %pad_maximum_fusion.2), channel_id=1, source_target_pairs={{0,120},{1,121},{120,0},{121,1},{2,122},{3,123},{122,2},{123,3},{4... | collective-permute-start | bytes 1572872 | tf_op jit(solution)/shard_map/ppermute | solution.py:259
  17.5 0.8 pad_maximum_fusion.1
  19.0 0.8 pad_maximum_fusion.3
  20.0 9.0 %all-to-all-done = bf16[32,128,128]{2,1,0:T(8,128)(2,1)} async-done(((bf16[32,128,128]{2,1,0:T(8,128)(2,1)}), bf16[32,128,128]{2,1,0:T(8,128)(2,1)}, u32[]{:S(2)}, u32[]{:S(2)}) %all-to-all-start) | async-done | bytes 1048608 | tf_op jit(solution)/shard_map/all_to_all | solution.py:264
  29.1 1.2 broadcast_in_dim.17
  30.3 4.8 %all-to-all-start.1 = ((bf16[32,128,128]{2,1,0:T(8,128)(2,1)}), bf16[32,128,128]{2,1,0:T(8,128)(2,1)}, u32[]{:S(2)}, u32[]{:S(2)}) async-start(bf16[32,128,128]{2,1,0:T(8,128)(2,1)} %bitcast.24), calls=%async_computation.1 | async-start | bytes 2097152 | tf_op jit(solution)/shard_map/all_to_all | solution.py:264
  35.0 4.8 %collective-permute-done.1.p2 = bf16[2,128,1024]{2,1,0:T(8,128)(2,1)S(1)} collective-permute-done((bf16[2,128,1024]{2,1,0:T(8,128)(2,1)}, bf16[2,128,1024]{2,1,0:T(8,128)(2,1)S(1)}, u32[]{:S(2)}, u32[]{:S(2)}) %collective-permute-start.1) | collective-permute-done | bytes 524320 | tf_op jit(solution)/shard_map/ppermute | solution.py:259
  39.9 19.0 %collective-permute-done.2.p3 = bf16[2,128,1024]{2,1,0:T(8,128)(2,1)S(1)} collective-permute-done((bf16[2,128,1024]{2,1,0:T(8,128)(2,1)}, bf16[2,128,1024]{2,1,0:T(8,128)(2,1)S(1)}, u32[]{:S(2)}, u32[]{:S(2)}) %collective-permute-start.2) | collective-permute-done | bytes 524320 | tf_op jit(solution)/shard_map/ppermute | solution.py:259
  58.8 24.9 %value_pass.1 = (bf16[16,256,128]{2,1,0:T(8,128)(2,1)}, f32[2,1,2048]{2,1,0:T(1,128)S(1)}) custom-call(s32[3]{0:T(128)S(1)} %pad_add_fusion.n_ref, bf16[2,128,1024]{2,1,0:T(8,128)(2,1)S(1)} %pad_maximum_fusion.p0, bf16[2,128,1024]{2,1,0:T(8,128)(2,1)S(1)} %collective-permute-done.p1, bf16[2,128,1024]{2,1,0:T(8,128)(2,1)S(1)} %collective-permute-done.1.p2, ...), custom_call_target="tpu_custom_call" | custom-call | flops 18253611008 | bytes 4194304 | tf_op jit(solution)/shard_map/value_pass/pallas_call | solution.py:198
  83.7 4.5 %all-to-all-start.3 = ((bf16[32,128,128]{2,1,0:T(8,128)(2,1)}), bf16[32,128,128]{2,1,0:T(8,128)(2,1)}, u32[]{:S(2)}, u32[]{:S(2)}) async-start(bf16[32,128,128]{2,1,0:T(8,128)(2,1)} %bitcast.15), calls=%async_computation.3 | async-start | bytes 2097152 | tf_op jit(solution)/shard_map/all_to_all | solution.py:264
  88.2 31.8 %key_pass.1 = (bf16[16,256,128]{2,1,0:T(8,128)(2,1)}, bf16[2,128,1024]{2,1,0:T(8,128)(2,1)S(1)}, bf16[2,128,1024]{2,1,0:T(8,128)(2,1)S(1)}, bf16[2,128,1024]{2,1,0:T(8,128)(2,1)S(1)}, bf16[2,128,1024]{2,1,0:T(8,128)(2,1)S(1)}) custom-call(s32[3]{0:T(128)S(1)} %pad_add_fusion.n_ref, bf16[2,128,1024]{2,1,0:T(8,128)(2,1)S(1)} %pad_maximum_fusion.p0, ...), custom_call_target="tpu_custom_call" | custom-call | flops 45634027520 | bytes 4194304 | tf_op jit(solution)/shard_map/key_pass/pallas_call | solution.py:224
  120.0 0.8 copy-done.1
  120.8 6.8 %all-to-all-start.2 = ((bf16[32,128,128]{2,1,0:T(8,128)(2,1)}), bf16[32,128,128]{2,1,0:T(8,128)(2,1)S(1)}, u32[]{:S(2)}, u32[]{:S(2)}) async-start(bf16[32,128,128]{2,1,0:T(8,128)(2,1)} %bitcast.27), calls=%async_computation.2 | async-start | bytes 2097152 | tf_op jit(solution)/shard_map/all_to_all | solution.py:264
  127.9 4.9 %collective-permute-start.4 = (bf16[2,128,1024]{2,1,0:T(8,128)(2,1)S(1)}, bf16[2,128,1024]{2,1,0:T(8,128)(2,1)S(1)}, u32[]{:S(2)}, u32[]{:S(2)}) collective-permute-start(bf16[2,128,1024]{2,1,0:T(8,128)(2,1)S(1)} %get-tuple-element.16), channel_id=1, source_target_pairs={{0,120},{1,121},{120,0},{121,1},{2,122},{3,123},{122,2},{123,3},{4... | collective-permute-start | bytes 1572872 | tf_op jit(solution)/shard_map/ppermute | solution.py:259
  133.2 22.7 %collective-permute-done.4.refs_2_ = bf16[2,128,1024]{2,1,0:T(8,128)(2,1)S(1)} collective-permute-done((bf16[2,128,1024]{2,1,0:T(8,128)(2,1)S(1)}, bf16[2,128,1024]{2,1,0:T(8,128)(2,1)S(1)}, u32[]{:S(2)}, u32[]{:S(2)}) %collective-permute-start.4) | collective-permute-done | bytes 524320 | tf_op jit(solution)/shard_map/ppermute | solution.py:259
  155.9 11.3 %collective-permute-done.5.refs_3_ = bf16[2,128,1024]{2,1,0:T(8,128)(2,1)S(1)} collective-permute-done((bf16[2,128,1024]{2,1,0:T(8,128)(2,1)S(1)}, bf16[2,128,1024]{2,1,0:T(8,128)(2,1)S(1)}, u32[]{:S(2)}, u32[]{:S(2)}) %collective-permute-start.5) | collective-permute-done | bytes 524320 | tf_op jit(solution)/shard_map/ppermute | solution.py:259
  167.1 2.4 %assemble.1 = (bf16[1,128,4096]{2,1,0:T(8,128)(2,1)}, f32[1,128,4096]{2,1,0:T(8,128)}) custom-call(s32[3]{0:T(128)S(1)} %pad_add_fusion.n_ref, bf16[2,128,1024]{2,1,0:T(8,128)(2,1)S(1)} %get-tuple-element.14.refs_0_, bf16[2,128,1024]{2,1,0:T(8,128)(2,1)S(1)} %collective-permute-done.3.refs_1_, bf16[2,128,1024]{2,1,0:T(8,128)(2,1)S(1)} %collective-permute-done.4.refs_2_, ...), custom_call_target="tpu_custom_call" | custom-call | tf_op jit(solution)/shard_map/assemble/pallas_call | solution.py:246
  169.5 1.4 convert_reduce_fusion
  171.1 0.8 copy.17
  172.2 0.8 copy.16
  (29 shorter events, 2.1 us)
Async XLA Ops:
  0.6 11.0 %copy-start.3 = (bf16[1,128,4096]{2,1,0:T(8,128)(2,1)S(1)}, bf16[1,128,4096]{2,1,0:T(8,128)(2,1)}, u32[]{:S(2)}) copy-start(bf16[1,128,4096]{2,1,0:T(8,128)(2,1)} %param.7) | copy-start | bytes 3145732
  0.6 11.0 %copy-start.4 = (bf16[1,128,4096]{2,1,0:T(8,128)(2,1)S(1)}, bf16[1,128,4096]{2,1,0:T(8,128)(2,1)}, u32[]{:S(2)}) copy-start(bf16[1,128,4096]{2,1,0:T(8,128)(2,1)} %param.4) | copy-start | bytes 3145732
  3.0 26.1 %all-to-all-start = ((bf16[32,128,128]{2,1,0:T(8,128)(2,1)}), bf16[32,128,128]{2,1,0:T(8,128)(2,1)}, u32[]{:S(2)}, u32[]{:S(2)}) async-start(bf16[32,128,128]{2,1,0:T(8,128)(2,1)} %bitcast.5), calls=%async_computation | async-start | bytes 2097152 | tf_op jit(solution)/shard_map/all_to_all | solution.py:264
  11.9 8.0 %copy-start.5 = (bf16[1,128,512]{2,1,0:T(8,128)(2,1)S(1)}, bf16[1,128,512]{2,1,0:T(8,128)(2,1)}, u32[]{:S(2)}) copy-start(bf16[1,128,512]{2,1,0:T(8,128)(2,1)} %param.6) | copy-start | bytes 393220
  12.7 27.1 %collective-permute-start.1 = (bf16[2,128,1024]{2,1,0:T(8,128)(2,1)}, bf16[2,128,1024]{2,1,0:T(8,128)(2,1)S(1)}, u32[]{:S(2)}, u32[]{:S(2)}) collective-permute-start(bf16[2,128,1024]{2,1,0:T(8,128)(2,1)} %pad_maximum_fusion.2), channel_id=1, source_target_pairs={{0,120},{1,121},{120,0},{121,1},{2,122},{3,123},{122,2},{123,3},{4... | collective-permute-start | bytes 1572872 | tf_op jit(solution)/shard_map/ppermute | solution.py:259
  18.4 21.5 %collective-permute-start = (bf16[2,128,1024]{2,1,0:T(8,128)(2,1)}, bf16[2,128,1024]{2,1,0:T(8,128)(2,1)S(1)}, u32[]{:S(2)}, u32[]{:S(2)}) collective-permute-start(bf16[2,128,1024]{2,1,0:T(8,128)(2,1)} %pad_maximum_fusion.1), channel_id=1, source_target_pairs={{0,1},{1,0},{120,121},{121,120},{2,3},{3,2},{122,123},{123,122},{4... | collective-permute-start | bytes 1572872 | tf_op jit(solution)/shard_map/ppermute | solution.py:259
  19.8 39.0 %collective-permute-start.2 = (bf16[2,128,1024]{2,1,0:T(8,128)(2,1)}, bf16[2,128,1024]{2,1,0:T(8,128)(2,1)S(1)}, u32[]{:S(2)}, u32[]{:S(2)}) collective-permute-start(bf16[2,128,1024]{2,1,0:T(8,128)(2,1)} %pad_maximum_fusion.3), channel_id=1, source_target_pairs={{0,121},{1,120},{120,1},{121,0},{2,123},{3,122},{122,3},{123,2},{4... | collective-permute-start | bytes 1572872 | tf_op jit(solution)/shard_map/ppermute | solution.py:259
  30.3 53.5 %all-to-all-start.1 = ((bf16[32,128,128]{2,1,0:T(8,128)(2,1)}), bf16[32,128,128]{2,1,0:T(8,128)(2,1)}, u32[]{:S(2)}, u32[]{:S(2)}) async-start(bf16[32,128,128]{2,1,0:T(8,128)(2,1)} %bitcast.24), calls=%async_computation.1 | async-start | bytes 2097152 | tf_op jit(solution)/shard_map/all_to_all | solution.py:264
  58.8 24.9 %copy-start = (bf16[2,128,1024]{2,1,0:T(8,128)(2,1)}, bf16[2,128,1024]{2,1,0:T(8,128)(2,1)S(1)}, u32[]{:S(2)}) copy-start(bf16[2,128,1024]{2,1,0:T(8,128)(2,1)S(1)} %collective-permute-done.2.p3) | copy-start | bytes 1572868
  83.7 37.1 %all-to-all-start.3 = ((bf16[32,128,128]{2,1,0:T(8,128)(2,1)}), bf16[32,128,128]{2,1,0:T(8,128)(2,1)}, u32[]{:S(2)}, u32[]{:S(2)}) async-start(bf16[32,128,128]{2,1,0:T(8,128)(2,1)} %bitcast.15), calls=%async_computation.3 | async-start | bytes 2097152 | tf_op jit(solution)/shard_map/all_to_all | solution.py:264
  120.0 0.8 copy-start.1
  120.8 6.8 %copy-start.2 = (bf16[2,128,1024]{2,1,0:T(8,128)(2,1)S(1)}, bf16[2,128,1024]{2,1,0:T(8,128)(2,1)}, u32[]{:S(2)}) copy-start(bf16[2,128,1024]{2,1,0:T(8,128)(2,1)} %copy-done.1) | copy-start | bytes 1572868
  120.8 51.1 %all-to-all-start.2 = ((bf16[32,128,128]{2,1,0:T(8,128)(2,1)}), bf16[32,128,128]{2,1,0:T(8,128)(2,1)S(1)}, u32[]{:S(2)}, u32[]{:S(2)}) async-start(bf16[32,128,128]{2,1,0:T(8,128)(2,1)} %bitcast.27), calls=%async_computation.2 | async-start | bytes 2097152 | tf_op jit(solution)/shard_map/all_to_all | solution.py:264
  127.6 5.5 %collective-permute-start.3 = (bf16[2,128,1024]{2,1,0:T(8,128)(2,1)S(1)}, bf16[2,128,1024]{2,1,0:T(8,128)(2,1)S(1)}, u32[]{:S(2)}, u32[]{:S(2)}) collective-permute-start(bf16[2,128,1024]{2,1,0:T(8,128)(2,1)S(1)} %copy-done.2), channel_id=1, source_target_pairs={{0,1},{1,0},{120,121},{121,120},{2,3},{3,2},{122,123},{123,122},{4... | collective-permute-start | bytes 1572872 | tf_op jit(solution)/shard_map/ppermute | solution.py:259
  127.9 28.0 %collective-permute-start.4 = (bf16[2,128,1024]{2,1,0:T(8,128)(2,1)S(1)}, bf16[2,128,1024]{2,1,0:T(8,128)(2,1)S(1)}, u32[]{:S(2)}, u32[]{:S(2)}) collective-permute-start(bf16[2,128,1024]{2,1,0:T(8,128)(2,1)S(1)} %get-tuple-element.16), channel_id=1, source_target_pairs={{0,120},{1,121},{120,0},{121,1},{2,122},{3,123},{122,2},{123,3},{4... | collective-permute-start | bytes 1572872 | tf_op jit(solution)/shard_map/ppermute | solution.py:259
  132.8 34.3 %collective-permute-start.5 = (bf16[2,128,1024]{2,1,0:T(8,128)(2,1)S(1)}, bf16[2,128,1024]{2,1,0:T(8,128)(2,1)S(1)}, u32[]{:S(2)}, u32[]{:S(2)}) collective-permute-start(bf16[2,128,1024]{2,1,0:T(8,128)(2,1)S(1)} %get-tuple-element.17), channel_id=1, source_target_pairs={{0,121},{1,120},{120,1},{121,0},{2,123},{3,122},{122,3},{123,2},{4... | collective-permute-start | bytes 1572872 | tf_op jit(solution)/shard_map/ppermute | solution.py:259
